TPU v7x, 128 devices: a whole 4x4x4 slice. The times are simulated.
128 devices in a mesh: lat: 32 (over y, z, core), fld: 4 (over x).
Axes of the slice: x: 4, y: 4, z: 4, core: 2. Of those that a mesh axis runs over, the one named last changes fastest.
Arguments:
- grid: bfloat16 [20, 32, 2, 5248], P('fld', 'lat'), may hold values from -6 to 6
- row_lengths: int32 [32], replicated, may hold values from 20 to 5136, as said below
- band_map: int32 [32], replicated, may hold values from 0 to 31, each once
- fold_map: int32 [128, 10], replicated, may hold values from 0 to 1279, as said below
- legendre: float32 [640, 1281, 32], P(('lat', 'fld')), may hold values from -0.75 to 0.75
- to_modes: float32 [20, 20], replicated, may hold values from -1.25 to 1.25
- back_modes: float32 [20, 20], replicated, may hold values from -1.25 to 1.25
- mode_rates: float32 [20], replicated, may hold values from 0.1 to 30
Outputs:
- spectral: float32 [20, 2, 640, 1281], P(None, None, ('lat', 'fld'))
- grid_out: bfloat16 [20, 32, 2, 5248], P('fld', 'lat')
Inputs may be any that keep to these rules, and one draw needn't show every extreme that they name: `row_lengths`: entry j is 20 + 4 i for an octahedral row index i with j * S <= i < (j + 1) * S, S = 40; entry 0 is 20 and the last entry is 5136; every entry is a multiple of 4. `fold_map`: every wavenumber 0 to 1279 stands exactly once; in every row, entries 2 s and 2 s + 1 are m and 1279 - m with m < 640. Row d lists the wavenumbers of the device with joined index d of lat+fld (lat index times the size of fld plus fld index). `band_map`: A permutation.
All inputs are finite; a program needn't handle non-finite values.
Results may differ from a plain program's by a relative error of at most 0.006.
Values sent between devices are 32-bit elements; how exact they have to be, the bound alone decides.
A program may use at most 64 MiB of HBM per device.

v0:
```python
import functools
import math

import jax
import jax.numpy as jnp
from jax import lax
from jax.experimental import pallas as pl
from jax.experimental.pallas import tpu as pltpu
from jax.sharding import PartitionSpec as P

HIGH = lax.Precision.HIGHEST
MESH = pl.DeviceIdType.MESH
F32, BF16, I32 = jnp.float32, jnp.bfloat16, jnp.int32
NT = (((1,), (1,)), ((), ()))

LAT, FLD = 32, 4
DEVS = LAT * FLD
FIELDS = 5
ALL_FIELDS = FIELDS * FLD
SLOTS = 10
PAIRS = SLOTS // 2
PLACES = 1281
CUT = 1279
WIDTH = 5248
WAVES = DEVS * SLOTS
ACROSS = 1296
STEP = 16
BLOCKS = ACROSS // STEP
LANES = 1408
CHUNK = 512
CHUNKS = 11


def iota(shape, dim):
    return lax.broadcasted_iota(I32, shape, dim)


def dot(a, b, precision=None):
    return jnp.dot(a, b, precision=precision, preferred_element_type=F32)


def dot_nt(a, b):
    return lax.dot_general(a, b, NT, preferred_element_type=F32)


SIN_TERMS = [(-1) ** k * math.pi ** (2 * k + 1) / math.factorial(2 * k + 1) for k in range(6)]
COS_TERMS = [(-1) ** k * math.pi ** (2 * k) / math.factorial(2 * k) for k in range(7)]


def horner(terms, square):
    total = jnp.full_like(square, terms[-1])
    for term in terms[-2::-1]:
        total = total * square + term
    return total


def turn(product, period, inverse):
    rest = product - period * jnp.round(product * inverse)
    part = rest * inverse
    square = part * part
    half_sin = part * horner(SIN_TERMS, square)
    half_cos = horner(COS_TERMS, square)
    return 1.0 - 2.0 * half_sin * half_sin, 2.0 * half_sin * half_cos


def split(value):
    upper = value.astype(BF16)
    return upper, (value - upper.astype(F32)).astype(BF16)


def row_of(value):
    return jnp.concatenate([value[s : s + 1] for s in range(SLOTS)], axis=1)


def kernel(
    len_ref, band_s_ref, fold_s_ref, fold_ref, band_ref, grid_ref, leg_ref, to_ref, back_ref, rate_ref,
    spec_ref, out_ref,
    cos_tab, sin_tab, wc_ref, ws_ref, sel_ref, leg4_ref, inv_ref, acc_c, acc_s, zc_ref, zs_ref, mat_ref, perm_ref, turned,
    send1, recv1, send2, recv2, sems,
):
    lat = lax.axis_index("lat")
    fld = lax.axis_index("fld")
    owner = lat * FLD + fld

    barrier = pltpu.get_barrier_semaphore()

    def greet(k, carry):
        other = lax.rem(owner + k, DEVS)
        pl.semaphore_signal(
            barrier, inc=1, device_id={"lat": other // FLD, "fld": lax.rem(other, FLD)}, device_id_type=MESH
        )
        return carry

    lax.fori_loop(1, DEVS, greet, 0)

    length = len_ref[band_s_ref[lat]]
    waves = row_of(fold_ref[...].astype(F32))
    full = jnp.full((1, WAVES), length.astype(F32), F32)
    quarter = full * 0.25
    inv_quarter = 1.0 / quarter
    scale = 1.0 / jnp.sqrt(full)
    keep = jnp.where(waves * 2.0 < full, 1.0, 0.0)
    zc, zs = turn(waves, full, 1.0 / full)
    zc_ref[...] = zc
    zs_ref[...] = zs

    base_c, base_s = turn(
        iota((STEP, WAVES), 0).astype(F32) * waves, quarter, inv_quarter
    )
    acc_c[0:STEP, :] = base_c
    acc_s[0:STEP, :] = base_s
    for start in range(0, 88, 8):
        c, s = turn((iota((8, WAVES), 0) + start).astype(F32) * (waves * float(STEP)), quarter, inv_quarter)
        wc_ref[start : start + 8, :] = c
        ws_ref[start : start + 8, :] = s

    def fill(j, carry):
        c, s = wc_ref[pl.ds(j, 1), :], ws_ref[pl.ds(j, 1), :]
        bc, bs = acc_c[0:STEP, :], acc_s[0:STEP, :]
        rows = pl.ds(pl.multiple_of(j * STEP, STEP), STEP)
        cos_tab[rows, :] = (bc * c - bs * s).astype(BF16)
        sin_tab[rows, :] = (bs * c + bc * s).astype(BF16)
        return carry

    lax.fori_loop(0, BLOCKS, fill, 0)

    column = iota((1, CHUNK), 1)
    target = (column & 127) * 4 + (column >> 7)
    sel_ref[...] = jnp.where(iota((CHUNK, CHUNK), 0) == target, 1.0, 0.0).astype(BF16)
    points = jnp.concatenate([grid_ref[f].astype(F32) for f in range(FIELDS)], axis=0)
    points = jnp.where(iota((2 * FIELDS, WIDTH), 1) < length, points, 0.0)
    points = jnp.concatenate([points, jnp.zeros((16 - 2 * FIELDS, WIDTH), F32)], axis=0).astype(BF16)
    points = jnp.concatenate([points, jnp.zeros((16, CHUNK * CHUNKS - WIDTH), BF16)], axis=1)
    points = jnp.concatenate([points[:, CHUNK * k : CHUNK * (k + 1)] for k in range(CHUNKS)], axis=0)
    points = dot(points, sel_ref[...]).astype(BF16)
    phases = jnp.concatenate(
        [
            jnp.concatenate([points[16 * k : 16 * (k + 1), 128 * b : 128 * (b + 1)] for k in range(CHUNKS)], axis=1)
            for b in range(4)
        ],
        axis=0,
    )[:, :ACROSS]

    acc_c[...] = dot(phases, cos_tab[...])
    acc_s[...] = dot(phases, sin_tab[...])
    re, im = acc_c[48:64, :], -acc_s[48:64, :]
    for b in (2, 1, 0):
        re, im = (
            re * zc + im * zs + acc_c[16 * b : 16 * (b + 1), :],
            im * zc - re * zs - acc_s[16 * b : 16 * (b + 1), :],
        )
    for c, part in enumerate((re, im)):
        part = part * (scale * keep)
        packed = jnp.concatenate(
            [part[0:10, 128 * s : 128 * (s + 1)] for s in range(SLOTS)] + [jnp.zeros((28, 128), F32)], axis=0
        )
        send1[:, c, :] = packed.T

    def exchange(source, dest, sem, row, row_at, back):
        def one(k, carry):
            other = lax.rem(owner + k, DEVS)
            o_lat, o_fld = other // FLD, lax.rem(other, FLD)
            pltpu.make_async_remote_copy(
                src_ref=source.at[row_at(o_lat, o_fld)],
                dst_ref=dest.at[row],
                send_sem=sems.at[sem],
                recv_sem=sems.at[sem + 1],
                device_id={"lat": o_lat, "fld": o_fld},
                device_id_type=MESH,
            ).start()
            return carry

        lax.fori_loop(1, DEVS, one, 0)
        dest[row] = source[row_at(lat, fld)]

    def finish(source, dest, sem):
        some = pl.ds(0, DEVS - 1)
        pltpu.make_async_copy(dest.at[some], dest.at[some], sems.at[sem + 1]).wait()
        pltpu.make_async_copy(source.at[some], source.at[some], sems.at[sem]).wait()

    pl.semaphore_wait(barrier, DEVS - 1)
    by_owner = lambda a, b: a * FLD + b
    by_group = lambda a, b: b * LAT + a
    exchange(send1, recv1, 0, by_group(lat, fld), by_owner, 0)

    place = iota((1, LANES), 1)
    for p in range(PAIRS):
        first = fold_s_ref[2 * p, owner]
        last = leg_ref[p, :, PLACES - 1 : PLACES]
        value = jnp.concatenate(
            [leg_ref[p, :, 0 : PLACES - 1], jnp.where(iota((LAT, 128), 1) == 0, last, 0.0)], axis=1
        )
        partner = place > CUT - first
        one = jnp.where(partner, 0.0, value)
        two = jnp.where(partner, value, 0.0)
        sign_one = jnp.where((place & 1) == 1, -1.0, 1.0)
        sign_two = jnp.where(((place + first) & 1) == 1, -1.0, 1.0)
        leg4_ref[p, 0:32, :] = one.astype(BF16)
        leg4_ref[p, 32:64, :] = (one * sign_one).astype(BF16)
        leg4_ref[p, 64:96, :] = two.astype(BF16)
        leg4_ref[p, 96:128, :] = (two * sign_two).astype(BF16)
        degree = jnp.where(partner, place - 1, first + place).astype(F32)
        tau = degree * (degree + 1.0) * (1.0 / float(CUT * (CUT + 1)))
        twice = jnp.where((iota((40, ALL_FIELDS), 0) >> 1) == iota((40, ALL_FIELDS), 1), rate_ref[...], 0.0)
        rates = jnp.sum(twice, axis=1, keepdims=True)
        inv_ref[p] = 1.0 / (1.0 + rates * tau)

    rows, cols = iota((40, 64), 0), iota((40, 64), 1)
    pick = jnp.where((iota((40, 20), 0) >> 1) == iota((40, 20), 1), 1.0, 0.0)
    spread_col = iota((20, 64), 1)
    spread = jnp.where(
        ((spread_col & 7) < FIELDS) & (iota((20, 64), 0) == (spread_col >> 4) * FIELDS + (spread_col & 7)), 1.0, 0.0
    )
    to_all = dot(dot(pick, to_ref[...], HIGH), spread, HIGH)
    to_all = jnp.where((rows & 1) == ((cols >> 3) & 1), to_all, 0.0)
    pick_t = jnp.where(iota((20, 40), 0) == (iota((20, 40), 1) >> 1), 1.0, 0.0)
    half = dot(back_ref[...], pick_t, HIGH)
    back_rows = dot(pick, half, HIGH)
    back_rows = jnp.where((iota((40, 40), 0) & 1) == (iota((40, 40), 1) & 1), back_rows, 0.0)
    back_upper, back_lower = split(back_rows)
    back_two = jnp.concatenate([back_upper.astype(F32), back_lower.astype(F32)], axis=0).astype(BF16)
    spread_row = iota((64, 20), 0)
    spread_t = jnp.where(
        ((spread_row & 7) < FIELDS) & (iota((64, 20), 1) == (spread_row >> 4) * FIELDS + (spread_row & 7)), 1.0, 0.0
    )
    back_all = dot(spread_t, half, HIGH)
    back_all = jnp.where(((iota((64, 40), 0) >> 3) & 1) == (iota((64, 40), 1) & 1), back_all, 0.0)
    bands = dot(band_ref[...].astype(F32), jnp.where(iota((LAT, 128), 0) == (iota((LAT, 128), 1) & 31), 1.0, 0.0), HIGH)
    bands = jnp.round(bands).astype(I32)
    square0, square1 = iota((128, 128), 0), iota((128, 128), 1)
    perm = jnp.where(((square0 & 31) == bands) & ((square0 >> 5) == (square1 >> 5)), 1.0, 0.0)

    finish(send1, recv1, 0)

    for c in range(2):
        turned[c] = recv1[:, c, :].T
    block = iota((16, 128), 1) >> 5
    gathered = []
    for p in range(PAIRS):
        rolled = []
        for j in range(4):
            at = 10 * (2 * p + (j >> 1)) + (j & 1)
            source = jnp.concatenate([turned[c, pl.ds(at, 8, stride=2), :] for c in range(2)], axis=0)
            rolled.append([source] + [pltpu.roll(source, 32 * k, 1) for k in range(1, 4)])
        parts = []
        for g in range(FLD):
            total = rolled[0][(0 - g) % 4]
            for j in range(1, 4):
                total = jnp.where(block == j, rolled[j][(j - g) % 4], total)
            parts.append(total)
        gathered.append(jnp.concatenate(parts, axis=0))
    modes_at = dot(to_all, jnp.concatenate(gathered, axis=1), HIGH)
    modes_at = jnp.concatenate([modes_at[:, 128 * p : 128 * (p + 1)] for p in range(PAIRS)], axis=0)
    modes_at = dot_nt(modes_at.astype(BF16), perm.astype(BF16))

    sums = []
    for p in range(PAIRS):
        modes = dot(modes_at[40 * p : 40 * (p + 1)].astype(BF16), leg4_ref[p])
        damped = (modes * inv_ref[p]).astype(BF16)
        sums.append(dot_nt(damped, leg4_ref[p]))
        spec = dot(back_two, damped)
        spec = spec[0:40] + spec[40:80]
        for g in range(ALL_FIELDS):
            spec_ref[g, p, :, :] = spec[2 * g : 2 * g + 2, 0:PLACES]

    returned = dot(back_all, jnp.concatenate(sums, axis=1), HIGH)
    returned = jnp.concatenate([returned[:, 128 * p : 128 * (p + 1)] for p in range(PAIRS)], axis=0)
    returned = dot(returned, perm, HIGH)
    turned[...] = jnp.zeros_like(turned)
    for p in range(PAIRS):
        rolled = []
        for g in range(FLD):
            source = returned[64 * p + 16 * g : 64 * p + 16 * (g + 1)]
            rolled.append([source] + [pltpu.roll(source, 32 * k, 1) for k in range(1, 4)])
        for j in range(4):
            total = rolled[0][(0 - j) % 4]
            for g in range(1, 4):
                total = jnp.where(block == g, rolled[g][(g - j) % 4], total)
            at = 10 * (2 * p + (j >> 1)) + (j & 1)
            for c in range(2):
                turned[c, pl.ds(at, 8, stride=2), :] = total[8 * c : 8 * (c + 1)]
    for c in range(2):
        send2[:, c, :] = turned[c].T
    exchange(send2, recv2, 2, by_owner(lat, fld), by_group, 0)
    finish(send2, recv2, 2)

    for c in range(2):
        turned[c] = recv2[:, c, :].T
    zc, zs = zc_ref[...], zs_ref[...]
    weight = keep * jnp.where(waves == 0.0, 1.0, 2.0)
    re, im = (
        jnp.concatenate([turned[c, 10 * s : 10 * s + 16, :] for s in range(SLOTS)], axis=1) * weight for c in range(2)
    )
    res, ims = [re], [im]
    for b in range(1, 4):
        re, im = re * zc - im * zs, re * zs + im * zc
        res.append(re)
        ims.append(im)
    total = dot_nt(jnp.concatenate(res, axis=0).astype(BF16), cos_tab[...])
    total = total - dot_nt(jnp.concatenate(ims, axis=0).astype(BF16), sin_tab[...])
    total = total * scale[:, 0:1]
    total = jnp.where(iota((64, ACROSS), 1) * 4 < length, total, 0.0)
    total = jnp.concatenate([total, jnp.zeros((64, LANES - ACROSS), F32)], axis=1).astype(BF16)
    total = jnp.concatenate(
        [
            jnp.concatenate([total[16 * b : 16 * (b + 1), 128 * k : 128 * (k + 1)] for b in range(4)], axis=1)
            for k in range(CHUNKS)
        ],
        axis=0,
    )
    total = dot_nt(total, sel_ref[...])
    total = jnp.concatenate([total[16 * k : 16 * (k + 1)] for k in range(CHUNKS)], axis=1)[:, :WIDTH]
    for f in range(FIELDS):
        out_ref[f, :, :] = total[2 * f : 2 * f + 2].astype(BF16)


def per_device(grid, row_lengths, band_map, fold_map, legendre, to_modes, back_modes, mode_rates):
    smem = pl.BlockSpec(memory_space=pltpu.SMEM)
    vmem = pl.BlockSpec(memory_space=pltpu.VMEM)
    fold_t = fold_map.T
    spectral, grid_out = pl.pallas_call(
        kernel,
        out_shape=(
            jax.ShapeDtypeStruct((ALL_FIELDS, PAIRS, 2, PLACES), F32),
            jax.ShapeDtypeStruct((FIELDS, 2, WIDTH), BF16),
        ),
        in_specs=[smem] * 3 + [vmem] * 7,
        out_specs=(vmem, vmem),
        scratch_shapes=[
            pltpu.VMEM((ACROSS, WAVES), BF16),
            pltpu.VMEM((ACROSS, WAVES), BF16),
            pltpu.VMEM((88, WAVES), F32),
            pltpu.VMEM((88, WAVES), F32),
            pltpu.VMEM((CHUNK, CHUNK), BF16),
            pltpu.VMEM((PAIRS, 128, LANES), BF16),
            pltpu.VMEM((PAIRS, 40, LANES), F32),
            pltpu.VMEM((64, WAVES), F32),
            pltpu.VMEM((64, WAVES), F32),
            pltpu.VMEM((1, WAVES), F32),
            pltpu.VMEM((1, WAVES), F32),
            pltpu.VMEM((8, 128), F32),
            pltpu.VMEM((128, 128), F32),
            pltpu.VMEM((2, 128, 128), F32),
            pltpu.VMEM((DEVS, 2, 128), F32),
            pltpu.VMEM((DEVS, 2, 128), F32),
            pltpu.VMEM((DEVS, 2, 128), F32),
            pltpu.VMEM((DEVS, 2, 128), F32),
            pltpu.SemaphoreType.DMA((4,)),
        ],
        compiler_params=pltpu.CompilerParams(
            collective_id=0, has_side_effects=True, vmem_limit_bytes=56 * 1024 * 1024
        ),
        name="spectral_transform",
    )(
        row_lengths,
        band_map,
        fold_t,
        fold_t,
        band_map.reshape(1, LAT),
        grid.reshape(FIELDS, 2, WIDTH),
        jnp.transpose(legendre, (0, 2, 1)),
        to_modes,
        back_modes,
        mode_rates.reshape(1, ALL_FIELDS),
    )
    return jnp.transpose(spectral, (0, 2, 1, 3)), grid_out.reshape(FIELDS, 1, 2, WIDTH)


def solution(mesh):
    placed = (
        P("fld", "lat", None, None),
        P(),
        P(),
        P(),
        P(("lat", "fld"), None, None),
        P(),
        P(),
        P(),
    )
    return jax.shard_map(
        per_device,
        mesh=mesh,
        in_specs=placed,
        out_specs=(P(None, None, ("lat", "fld"), None), P("fld", "lat", None, None)),
        check_vma=False,
    )
```

profile of v0, /device:TPU:1, one launch (start us, length us, event | category | flops | bytes accessed | tf_op | source)
XLA Modules:
  0.0 37.1 jit_solution(7570190785328723350)
XLA Ops:
  0.6 33.4 %spectral_transform.1 = (f32[20,5,2,1281]{3,2,1,0:T(2,128)}, bf16[5,2,5248]{2,1,0:T(2,128)(2,1)}) custom-call(s32[32]{0:T(128)} %len_ref.1, s32[32]{0:T(128)} %band_s_ref.1, s32[10,128]{1,0:T(8,128)} %bitcast.13, s32[10,128]{1,0:T(8,128)} %bitcast.14, s32[1,32]{1,0:T(1,128)} %bitcast.15, bf16[5,2,5248]{2,1,0:T(2,128)(2,1)} %bitcast.12, ...), custom_call_target="tpu_custom_call" | custom-call | tf_op jit(solution)/shard_map/spectral_transform/pallas_call | solution.py:321
  34.0 0.0 copy-start
  34.0 2.4 %copy.13 = f32[20,2,5,1281]{3,1,2,0:T(2,128)} copy(f32[20,2,5,1281]{3,1,2,0:T(2,128)} %bitcast.9) | data formatting | bytes 2049600
  36.4 0.0 copy-done
  36.4 0.6 %copy.14 = bf16[5,1,2,5248]{3,2,1,0:T(2,128)(2,1)} copy(bf16[5,1,2,5248]{3,2,1,0:T(2,128)(2,1)S(1)} %bitcast.11) | data formatting | bytes 209920
Async XLA Ops:
  34.0 2.4 %copy-start = (bf16[5,2,5248]{2,1,0:T(2,128)(2,1)S(1)}, bf16[5,2,5248]{2,1,0:T(2,128)(2,1)}, u32[]{:S(2)}) copy-start(bf16[5,2,5248]{2,1,0:T(2,128)(2,1)} %get-tuple-element.5) | copy-start | bytes 314884
where the time goes:
time: 37.2 us; the launch traced here: 37.1 us
  Pallas kernels  33.4 us (90%)
  local copies, waits for them, and re-layouts  3.05 us (8%)
  between operations  0.65 us (2%)
    pallas_call x1, Pallas kernels, per_device(): pl.pallas_call(kernel, out_shape=(jax.ShapeDtypeStruct((ALL_FIELDS, PAIRS...  33.4 us
    unnamed x4, local copies, waits for them, and re-layouts  3.05 us

commit v1 on v0

v1 whole, which is shorter than its diff:
```python
import functools
import math

import jax
import jax.numpy as jnp
from jax import lax
from jax.experimental import pallas as pl
from jax.experimental.pallas import tpu as pltpu
from jax.sharding import PartitionSpec as P

HIGH = lax.Precision.HIGHEST
MESH = pl.DeviceIdType.MESH
F32, BF16, I32 = jnp.float32, jnp.bfloat16, jnp.int32
NT = (((1,), (1,)), ((), ()))

LAT, FLD = 32, 4
DEVS = LAT * FLD
FIELDS = 5
ALL_FIELDS = FIELDS * FLD
SLOTS = 10
PAIRS = SLOTS // 2
PLACES = 1281
CUT = 1279
WIDTH = 5248
WAVES = DEVS * SLOTS
ACROSS = 1296
STEP = 16
BLOCKS = ACROSS // STEP
LANES = 1408
CHUNK = 512
CHUNKS = 11


def iota(shape, dim):
    return lax.broadcasted_iota(I32, shape, dim)


def dot(a, b, precision=None):
    return jnp.dot(a, b, precision=precision, preferred_element_type=F32)


def dot_nt(a, b):
    return lax.dot_general(a, b, NT, preferred_element_type=F32)


SIN_TERMS = [(-1) ** k * math.pi ** (2 * k + 1) / math.factorial(2 * k + 1) for k in range(6)]
COS_TERMS = [(-1) ** k * math.pi ** (2 * k) / math.factorial(2 * k) for k in range(7)]


def horner(terms, square):
    total = jnp.full_like(square, terms[-1])
    for term in terms[-2::-1]:
        total = total * square + term
    return total


def turn(product, period, inverse):
    rest = product - period * jnp.round(product * inverse)
    part = rest * inverse
    square = part * part
    half_sin = part * horner(SIN_TERMS, square)
    half_cos = horner(COS_TERMS, square)
    return 1.0 - 2.0 * half_sin * half_sin, 2.0 * half_sin * half_cos


def row_of(value):
    return jnp.concatenate([value[s : s + 1] for s in range(SLOTS)], axis=1)


def split(value):
    upper = value.astype(BF16)
    return upper, (value - upper.astype(F32)).astype(BF16)


def offsets():
    hops = (0, 1, 2, 1)
    steps = [(x, y, z, c) for y in range(4) for z in range(4) for c in range(2) for x in range(4)][1:]
    return sorted(steps, key=lambda step: -(hops[step[0]] + hops[step[1]] + hops[step[2]]))


def send_kernel(
    len_hbm, band_s_hbm, fold_hbm, band_hbm, grid_hbm, leg_hbm, to_hbm, back_hbm, rate_hbm,
    spec_ref, cos_tab, sin_tab, tre_ref, tim_ref, size_ref,
    len_ref, band_s_ref, fold_s_ref, fold_ref, band_ref, grid_ref, leg_ref, to_ref, back_ref, rate_ref,
    wc_ref, ws_ref, leg4_ref, inv_ref, damp_ref, acc_c, acc_s, turned,
    send1, recv1, send2, recv2, in_sems, sems,
):
    lat = lax.axis_index("lat")
    fld = lax.axis_index("fld")
    owner = lat * FLD + fld

    moves = [
        pltpu.make_async_copy(source, dest, in_sems.at[k])
        for k, (source, dest) in enumerate(
            (
                (len_hbm, len_ref), (band_s_hbm, band_s_ref), (fold_hbm, fold_ref), (grid_hbm, grid_ref),
                (fold_hbm, fold_s_ref), (band_hbm, band_ref), (to_hbm, to_ref), (back_hbm, back_ref),
                (rate_hbm, rate_ref), (leg_hbm, leg_ref),
            )
        )
    ]
    for move in moves:
        move.start()

    high, middle, core = lat // 8, lax.rem(lat // 2, 4), lax.rem(lat, 2)
    xs, ys, zs_, cs = (
        [at] + [lax.rem(at + k, size) for k in range(1, size)]
        for at, size in ((fld, 4), (high, 4), (middle, 4), (core, 2))
    )
    peers = [(ys[y] * 8 + zs_[z] * 2 + cs[c], xs[x]) for x, y, z, c in offsets()]

    barrier = pltpu.get_barrier_semaphore()
    for o_lat, o_fld in peers:
        pl.semaphore_signal(barrier, inc=1, device_id={"lat": o_lat, "fld": o_fld}, device_id_type=MESH)

    for move in moves[:4]:
        move.wait()
    length = len_ref[band_s_ref[lat]]
    waves = row_of(fold_ref[...].astype(F32))
    full = jnp.full((1, WAVES), length.astype(F32), F32)
    size_ref[...] = jnp.full((8, 128), length.astype(F32), F32)
    quarter = full * 0.25
    inv_quarter = 1.0 / quarter
    scale = 1.0 / jnp.sqrt(full)
    keep = jnp.where(waves * 2.0 < full, 1.0, 0.0)
    zc, zs = turn(waves, full, 1.0 / full)

    base_c, base_s = turn(
        iota((STEP, WAVES), 0).astype(F32) * waves, quarter, inv_quarter
    )
    acc_c[0:STEP, :] = base_c
    acc_s[0:STEP, :] = base_s
    for start in range(0, 88, 8):
        c, s = turn((iota((8, WAVES), 0) + start).astype(F32) * (waves * float(STEP)), quarter, inv_quarter)
        wc_ref[start : start + 8, :] = c
        ws_ref[start : start + 8, :] = s

    def fill(j, carry):
        c, s = wc_ref[pl.ds(j, 1), :], ws_ref[pl.ds(j, 1), :]
        bc, bs = acc_c[0:STEP, :], acc_s[0:STEP, :]
        rows = pl.ds(pl.multiple_of(j * STEP, STEP), STEP)
        cos_tab[rows, :] = (bc * c - bs * s).astype(BF16)
        sin_tab[rows, :] = (bs * c + bc * s).astype(BF16)
        return carry

    lax.fori_loop(0, BLOCKS, fill, 0)

    points = jnp.concatenate([grid_ref[f].astype(F32) for f in range(FIELDS)], axis=0)
    points = jnp.where(iota((2 * FIELDS, WIDTH), 1) < length, points, 0.0)
    points = jnp.concatenate([points, jnp.zeros((16 - 2 * FIELDS, WIDTH), F32)], axis=0).astype(BF16)
    points = jnp.concatenate([points, jnp.zeros((16, CHUNK * CHUNKS - WIDTH), BF16)], axis=1)
    points = jnp.concatenate([points[:, CHUNK * k : CHUNK * (k + 1)] for k in range(CHUNKS)], axis=0)
    points = dot(points, selection()).astype(BF16)
    phases = jnp.concatenate(
        [
            jnp.concatenate([points[16 * k : 16 * (k + 1), 128 * b : 128 * (b + 1)] for k in range(CHUNKS)], axis=1)
            for b in range(4)
        ],
        axis=0,
    )[:, :ACROSS]

    acc_c[...] = dot(phases, cos_tab[...])
    acc_s[...] = dot(phases, sin_tab[...])
    re, im = acc_c[48:64, :], -acc_s[48:64, :]
    for b in (2, 1, 0):
        re, im = (
            re * zc + im * zs + acc_c[16 * b : 16 * (b + 1), :],
            im * zc - re * zs - acc_s[16 * b : 16 * (b + 1), :],
        )
    for c, part in enumerate((re, im)):
        part = part * (scale * keep)
        packed = jnp.concatenate(
            [part[0:10, 128 * s : 128 * (s + 1)] for s in range(SLOTS)] + [jnp.zeros((28, 128), F32)], axis=0
        )
        send1[:, c, :] = packed.T

    for move in moves[4:]:
        move.wait()
    perm = jnp.where(iota((LAT, LAT), 0) == band_ref[...], 1.0, 0.0).astype(BF16)
    rates = jnp.sum(
        jnp.where((iota((40, ALL_FIELDS), 0) >> 1) == iota((40, ALL_FIELDS), 1), rate_ref[...], 0.0),
        axis=1, keepdims=True,
    )
    place = iota((1, LANES), 1)
    for p in range(PAIRS):
        first = fold_s_ref[2 * p, owner]
        last = leg_ref[p, :, PLACES - 1 : PLACES]
        value = jnp.concatenate(
            [leg_ref[p, :, 0 : PLACES - 1], jnp.where(iota((LAT, 128), 1) == 0, last, 0.0)], axis=1
        )
        value = lax.dot_general(perm, value.astype(BF16), (((0,), (0,)), ((), ())), preferred_element_type=F32)
        partner = place > CUT - first
        one = jnp.where(partner, 0.0, value)
        two = jnp.where(partner, value, 0.0)
        sign_one = jnp.where((place & 1) == 1, -1.0, 1.0)
        sign_two = jnp.where(((place + first) & 1) == 1, -1.0, 1.0)
        leg4_ref[p, 0:32, :] = one.astype(BF16)
        leg4_ref[p, 32:64, :] = (one * sign_one).astype(BF16)
        leg4_ref[p, 64:96, :] = two.astype(BF16)
        leg4_ref[p, 96:128, :] = (two * sign_two).astype(BF16)
        degree = jnp.where(partner, place - 1, first + place).astype(F32)
        tau = degree * (degree + 1.0) * (1.0 / float(CUT * (CUT + 1)))
        inv_ref[p] = 1.0 / (1.0 + rates * tau)

    rows, cols = iota((40, 64), 0), iota((40, 64), 1)
    pick = jnp.where((iota((40, 20), 0) >> 1) == iota((40, 20), 1), 1.0, 0.0)
    spread_col = iota((20, 64), 1)
    spread = jnp.where(
        ((spread_col & 7) < FIELDS) & (iota((20, 64), 0) == (spread_col >> 4) * FIELDS + (spread_col & 7)), 1.0, 0.0
    )
    to_all = dot(dot(pick, to_ref[...], HIGH), spread, HIGH)
    to_all = jnp.where((rows & 1) == ((cols >> 3) & 1), to_all, 0.0)
    pick_t = jnp.where(iota((20, 40), 0) == (iota((20, 40), 1) >> 1), 1.0, 0.0)
    half = dot(back_ref[...], pick_t, HIGH)
    back_rows = dot(pick, half, HIGH)
    back_rows = jnp.where((iota((40, 40), 0) & 1) == (iota((40, 40), 1) & 1), back_rows, 0.0)
    back_upper, back_lower = split(back_rows)
    back_two = jnp.concatenate([back_upper.astype(F32), back_lower.astype(F32)], axis=0).astype(BF16)
    spread_row = iota((64, 20), 0)
    spread_t = jnp.where(
        ((spread_row & 7) < FIELDS) & (iota((64, 20), 1) == (spread_row >> 4) * FIELDS + (spread_row & 7)), 1.0, 0.0
    )
    back_all = dot(spread_t, half, HIGH)
    back_all = jnp.where(((iota((64, 40), 0) >> 3) & 1) == (iota((64, 40), 1) & 1), back_all, 0.0)

    def exchange(source, dest, sem, row, row_at):
        for o_lat, o_fld in peers:
            pltpu.make_async_remote_copy(
                src_ref=source.at[row_at(o_lat, o_fld)],
                dst_ref=dest.at[row],
                send_sem=sems.at[sem],
                recv_sem=sems.at[sem + 1],
                device_id={"lat": o_lat, "fld": o_fld},
                device_id_type=MESH,
            ).start()
        dest[row] = source[row_at(lat, fld)]

    def finish(buffer, sem):
        some = buffer.at[pl.ds(0, DEVS - 1)]
        pltpu.make_async_copy(some, some, sems.at[sem]).wait()

    by_owner = lambda a, b: a * FLD + b
    by_group = lambda a, b: b * LAT + a
    pl.semaphore_wait(barrier, DEVS - 1)
    exchange(send1, recv1, 0, by_group(lat, fld), by_owner)
    finish(recv1, 1)

    for c in range(2):
        turned[c] = recv1[:, c, :].T
    block = iota((16, 128), 1) >> 5
    gathered = []
    for p in range(PAIRS):
        rolled = []
        for j in range(4):
            at = 10 * (2 * p + (j >> 1)) + (j & 1)
            source = jnp.concatenate([turned[c, pl.ds(at, 8, stride=2), :] for c in range(2)], axis=0)
            rolled.append([source] + [pltpu.roll(source, 32 * k, 1) for k in range(1, 4)])
        parts = []
        for g in range(FLD):
            total = rolled[0][(0 - g) % 4]
            for j in range(1, 4):
                total = jnp.where(block == j, rolled[j][(j - g) % 4], total)
            parts.append(total)
        gathered.append(jnp.concatenate(parts, axis=0))
    modes_at = dot(to_all, jnp.concatenate(gathered, axis=1), HIGH).astype(BF16)

    sums = []
    for p in range(PAIRS):
        modes = dot(modes_at[:, 128 * p : 128 * (p + 1)], leg4_ref[p])
        damped = (modes * inv_ref[p]).astype(BF16)
        damp_ref[p, 0:40, :] = damped
        sums.append(dot_nt(damped, leg4_ref[p]))

    returned = dot(back_all, jnp.concatenate(sums, axis=1), HIGH)
    turned[...] = jnp.zeros_like(turned)
    for p in range(PAIRS):
        rolled = []
        for g in range(FLD):
            source = returned[16 * g : 16 * (g + 1), 128 * p : 128 * (p + 1)]
            rolled.append([source] + [pltpu.roll(source, 32 * k, 1) for k in range(1, 4)])
        for j in range(4):
            total = rolled[0][(0 - j) % 4]
            for g in range(1, 4):
                total = jnp.where(block == g, rolled[g][(g - j) % 4], total)
            at = 10 * (2 * p + (j >> 1)) + (j & 1)
            for c in range(2):
                turned[c, pl.ds(at, 8, stride=2), :] = total[8 * c : 8 * (c + 1)]
    for c in range(2):
        send2[:, c, :] = turned[c].T
    exchange(send2, recv2, 2, by_owner(lat, fld), by_group)

    for p in range(PAIRS):
        spec = dot(back_two, damp_ref[p, 0:40, :])
        spec = spec[0:40] + spec[40:80]
        for g in range(ALL_FIELDS):
            spec_ref[g, p, :, :] = spec[2 * g : 2 * g + 2, 0:PLACES]

    finish(recv2, 3)

    for c in range(2):
        turned[c] = recv2[:, c, :].T
    weight = keep * jnp.where(waves == 0.0, 1.0, 2.0)
    re, im = (
        jnp.concatenate([turned[c, 10 * s : 10 * s + 16, :] for s in range(SLOTS)], axis=1) * weight for c in range(2)
    )
    for b in range(4):
        tre_ref[16 * b : 16 * (b + 1), :] = re.astype(BF16)
        tim_ref[16 * b : 16 * (b + 1), :] = im.astype(BF16)
        if b < 3:
            re, im = re * zc - im * zs, re * zs + im * zc
    finish(send1, 0)
    finish(send2, 2)


def points_kernel(spec_in, cos_tab, sin_tab, tre_ref, tim_ref, size_ref, spec_out, out_ref, sem):
    move = pltpu.make_async_copy(spec_in, spec_out, sem)
    move.start()
    length = size_ref[0:1, 0:1]
    scale = 1.0 / jnp.sqrt(length)
    total = dot_nt(tre_ref[...], cos_tab[...]) - dot_nt(tim_ref[...], sin_tab[...])
    total = total * scale
    total = jnp.where((iota((64, ACROSS), 1) * 4).astype(F32) < length, total, 0.0)
    total = jnp.concatenate([total, jnp.zeros((64, LANES - ACROSS), F32)], axis=1).astype(BF16)
    total = jnp.concatenate(
        [
            jnp.concatenate([total[16 * b : 16 * (b + 1), 128 * k : 128 * (k + 1)] for b in range(4)], axis=1)
            for k in range(CHUNKS)
        ],
        axis=0,
    )
    total = dot_nt(total, selection())
    total = jnp.concatenate([total[16 * k : 16 * (k + 1)] for k in range(CHUNKS)], axis=1)[:, :WIDTH]
    for f in range(FIELDS):
        out_ref[f, :, :] = total[2 * f : 2 * f + 2].astype(BF16)
    move.wait()


def selection():
    column = iota((1, CHUNK), 1)
    target = (column & 127) * 4 + (column >> 7)
    return jnp.where(iota((CHUNK, CHUNK), 0) == target, 1.0, 0.0).astype(BF16)


def per_device(grid, row_lengths, band_map, fold_map, legendre, to_modes, back_modes, mode_rates):
    vmem = pl.BlockSpec(memory_space=pltpu.VMEM)
    anywhere = pl.BlockSpec(memory_space=pl.ANY)
    spec_shape = (ALL_FIELDS, PAIRS, 2, PLACES)
    held = pl.pallas_call(
        send_kernel,
        out_shape=(
            pltpu.VMEM(spec_shape, F32),
            pltpu.VMEM((ACROSS, WAVES), BF16),
            pltpu.VMEM((ACROSS, WAVES), BF16),
            pltpu.VMEM((64, WAVES), BF16),
            pltpu.VMEM((64, WAVES), BF16),
            pltpu.VMEM((8, 128), F32),
        ),
        in_specs=[pl.BlockSpec(memory_space=pltpu.HBM)] * 9,
        out_specs=(vmem,) * 6,
        scratch_shapes=[
            pltpu.SMEM((LAT,), I32),
            pltpu.SMEM((LAT,), I32),
            pltpu.SMEM((SLOTS, DEVS), I32),
            pltpu.VMEM((SLOTS, DEVS), I32),
            pltpu.VMEM((1, LAT), I32),
            pltpu.VMEM((FIELDS, 2, WIDTH), BF16),
            pltpu.VMEM((PAIRS, LAT, PLACES), F32),
            pltpu.VMEM((ALL_FIELDS, ALL_FIELDS), F32),
            pltpu.VMEM((ALL_FIELDS, ALL_FIELDS), F32),
            pltpu.VMEM((1, ALL_FIELDS), F32),
            pltpu.VMEM((88, WAVES), F32),
            pltpu.VMEM((88, WAVES), F32),
            pltpu.VMEM((PAIRS, 128, LANES), BF16),
            pltpu.VMEM((PAIRS, 40, LANES), F32),
            pltpu.VMEM((PAIRS, 48, LANES), BF16),
            pltpu.VMEM((64, WAVES), F32),
            pltpu.VMEM((64, WAVES), F32),
            pltpu.VMEM((2, 128, 128), F32),
            pltpu.VMEM((DEVS, 2, 128), F32),
            pltpu.VMEM((DEVS, 2, 128), F32),
            pltpu.VMEM((DEVS, 2, 128), F32),
            pltpu.VMEM((DEVS, 2, 128), F32),
            pltpu.SemaphoreType.DMA((10,)),
            pltpu.SemaphoreType.DMA((4,)),
        ],
        compiler_params=pltpu.CompilerParams(
            collective_id=0, has_side_effects=True, vmem_limit_bytes=24 * 1024 * 1024
        ),
        name="to_spectral",
    )(
        *[
            pltpu.with_memory_space_constraint(value, pltpu.HBM)
            for value in (
                row_lengths,
                band_map,
                fold_map.T,
                band_map.reshape(1, LAT),
                grid.reshape(FIELDS, 2, WIDTH),
                jnp.transpose(legendre, (0, 2, 1)),
                to_modes,
                back_modes,
                mode_rates.reshape(1, ALL_FIELDS),
            )
        ]
    )
    held = [pltpu.with_memory_space_constraint(value, pltpu.VMEM) for value in held]
    spectral, grid_out = pl.pallas_call(
        points_kernel,
        out_shape=(
            jax.ShapeDtypeStruct(spec_shape, F32),
            jax.ShapeDtypeStruct((FIELDS, 2, WIDTH), BF16),
        ),
        in_specs=[vmem] * 6,
        out_specs=(anywhere, vmem),
        scratch_shapes=[pltpu.SemaphoreType.DMA],
        compiler_params=pltpu.CompilerParams(vmem_limit_bytes=24 * 1024 * 1024),
        name="to_points",
    )(*held)
    return jnp.transpose(spectral, (0, 2, 1, 3)), grid_out.reshape(FIELDS, 1, 2, WIDTH)


def solution(mesh):
    placed = (
        P("fld", "lat", None, None),
        P(),
        P(),
        P(),
        P(("lat", "fld"), None, None),
        P(),
        P(),
        P(),
    )
    return jax.shard_map(
        per_device,
        mesh=mesh,
        in_specs=placed,
        out_specs=(P(None, None, ("lat", "fld"), None), P("fld", "lat", None, None)),
        check_vma=False,
    )
```

time: 37.2 us -> 29.6 us (0.80)
  Pallas kernels: 33.4 us -> 28.8 us
  local copies, waits for them, and re-layouts: 3.05 us -> 0 us
    pallas_call x1 -> x2, Pallas kernels: 33.4 us -> 28.8 us  [the longest x1 25.9 us: per_device(): pl.pallas_call(send_kernel, out_shape=(pltpu.VMEM(spec_shape, F32), pltpu...]
    unnamed x4 -> x0, local copies, waits for them, and re-layouts: 3.05 us -> none
where the time goes in v1:
time: 29.6 us; the launch traced here: 29.5 us
  Pallas kernels  28.8 us (97%)
  between operations  0.64 us (2%)
    pallas_call x1, Pallas kernels, per_device(): pl.pallas_call(send_kernel, out_shape=(pltpu.VMEM(spec_shape, F32), pltpu...  25.9 us
    pallas_call x1, Pallas kernels, per_device(): pl.pallas_call(points_kernel, out_shape=(jax.ShapeDtypeStruct(spec_shape,...  2.91 us

profile of v1, /device:TPU:1, one launch (start us, length us, event | category | flops | bytes accessed | tf_op | source)
XLA Modules:
  0.0 29.5 jit_solution(1355968474315739091)
XLA Ops:
  0.6 25.9 %to_spectral.1 = (f32[20,5,2,1281]{3,2,1,0:T(2,128)S(1)}, bf16[1296,1280]{1,0:T(8,128)(2,1)S(1)}, bf16[1296,1280]{1,0:T(8,128)(2,1)S(1)}, bf16[64,1280]{1,0:T(8,...) custom-call(s32[32]{0:T(128)} %len_hbm.1, s32[32]{0:T(128)} %band_s_hbm.1, s32[10,128]{1,0:T(8,128)} %bitcast.11, ...), custom_call_target="tpu_custom_call" | custom-call | tf_op jit(solution)/shard_map/to_spectral/pallas_call | solution.py:348
  26.6 2.9 %to_points.1 = (f32[20,5,2,1281]{3,2,1,0:T(2,128)}, bf16[5,2,5248]{2,1,0:T(2,128)(2,1)}) custom-call(f32[20,5,2,1281]{3,2,1,0:T(2,128)S(1)} %get-tuple-element.10.spec_in, bf16[1296,1280]{1,0:T(8,128)(2,1)S(1)} %get-tuple-element.11.cos_tab, bf16[1296,1280]{1,0:T(8,128)(2,1)S(1)} %get-tuple-element.12.sin_tab, ...), custom_call_target="tpu_custom_call" | custom-call | tf_op jit(solution)/shard_map/to_points/pallas_call | solution.py:407

commit v2 on v1

--- a/solution.py
+++ b/solution.py
@@ -23,9 +23,11 @@
 CUT = 1279
 WIDTH = 5248
 WAVES = DEVS * SLOTS
-ACROSS = 1296
+HALF = 672
+GROUP = 256
+UNROLL = 2
 STEP = 16
-BLOCKS = ACROSS // STEP
+BLOCKS = HALF // STEP
 LANES = 1408
 CHUNK = 512
 CHUNKS = 11
@@ -72,6 +74,12 @@
     return upper, (value - upper.astype(F32)).astype(BF16)
 
 
+def dot_split(left, right):
+    left_upper, left_lower = split(left)
+    right_upper, right_lower = split(right)
+    return dot(left_upper, right_upper) + (dot(left_upper, right_lower) + dot(left_lower, right_upper))
+
+
 def offsets():
     hops = (0, 1, 2, 1)
     steps = [(x, y, z, c) for y in range(4) for z in range(4) for c in range(2) for x in range(4)][1:]
@@ -80,9 +88,9 @@
 
 def send_kernel(
     len_hbm, band_s_hbm, fold_hbm, band_hbm, grid_hbm, leg_hbm, to_hbm, back_hbm, rate_hbm,
-    spec_ref, cos_tab, sin_tab, tre_ref, tim_ref, size_ref,
+    spec_ref, cos_tab, sin_tab, tre_ref, tim_ref, size_ref, sel_ref,
     len_ref, band_s_ref, fold_s_ref, fold_ref, band_ref, grid_ref, leg_ref, to_ref, back_ref, rate_ref,
-    wc_ref, ws_ref, leg4_ref, inv_ref, damp_ref, acc_c, acc_s, turned,
+    wc_ref, ws_ref, rev_ref, leg4_ref, inv_ref, damp_ref, acc_c, acc_s, turned,
     send1, recv1, send2, recv2, in_sems, sems,
 ):
     lat = lax.axis_index("lat")
@@ -113,54 +121,63 @@
     for o_lat, o_fld in peers:
         pl.semaphore_signal(barrier, inc=1, device_id={"lat": o_lat, "fld": o_fld}, device_id_type=MESH)
 
+    sel_ref[...] = selection(False)
+    rev_ref[...] = selection(True)
+
     for move in moves[:4]:
         move.wait()
     length = len_ref[band_s_ref[lat]]
     waves = row_of(fold_ref[...].astype(F32))
     full = jnp.full((1, WAVES), length.astype(F32), F32)
-    size_ref[...] = jnp.full((8, 128), length.astype(F32), F32)
+    size_ref[...] = jnp.full((8, 128), length, I32)
     quarter = full * 0.25
     inv_quarter = 1.0 / quarter
     scale = 1.0 / jnp.sqrt(full)
     keep = jnp.where(waves * 2.0 < full, 1.0, 0.0)
     zc, zs = turn(waves, full, 1.0 / full)
 
-    base_c, base_s = turn(
-        iota((STEP, WAVES), 0).astype(F32) * waves, quarter, inv_quarter
-    )
-    acc_c[0:STEP, :] = base_c
-    acc_s[0:STEP, :] = base_s
-    for start in range(0, 88, 8):
+    base_c, base_s = turn(iota((STEP, WAVES), 0).astype(F32) * waves, quarter, inv_quarter)
+    for start in range(0, 48, 8):
         c, s = turn((iota((8, WAVES), 0) + start).astype(F32) * (waves * float(STEP)), quarter, inv_quarter)
         wc_ref[start : start + 8, :] = c
         ws_ref[start : start + 8, :] = s
-
-    def fill(j, carry):
-        c, s = wc_ref[pl.ds(j, 1), :], ws_ref[pl.ds(j, 1), :]
-        bc, bs = acc_c[0:STEP, :], acc_s[0:STEP, :]
-        rows = pl.ds(pl.multiple_of(j * STEP, STEP), STEP)
-        cos_tab[rows, :] = (bc * c - bs * s).astype(BF16)
-        sin_tab[rows, :] = (bs * c + bc * s).astype(BF16)
-        return carry
-
-    lax.fori_loop(0, BLOCKS, fill, 0)
+    for start in range(0, WAVES, GROUP):
+        lanes = slice(start, start + GROUP)
+        bc, bs = base_c[:, lanes], base_s[:, lanes]
+
+        def fill(j, carry):
+            c, s = wc_ref[pl.ds(j, 1), lanes], ws_ref[pl.ds(j, 1), lanes]
+            rows = pl.ds(pl.multiple_of(j * STEP, STEP), STEP)
+            cos_tab[rows, lanes] = (bc * c - bs * s).astype(BF16)
+            sin_tab[rows, lanes] = (bs * c + bc * s).astype(BF16)
+            return carry
+
+        lax.fori_loop(0, BLOCKS, fill, 0, unroll=UNROLL)
 
     points = jnp.concatenate([grid_ref[f].astype(F32) for f in range(FIELDS)], axis=0)
     points = jnp.where(iota((2 * FIELDS, WIDTH), 1) < length, points, 0.0)
     points = jnp.concatenate([points, jnp.zeros((16 - 2 * FIELDS, WIDTH), F32)], axis=0).astype(BF16)
     points = jnp.concatenate([points, jnp.zeros((16, CHUNK * CHUNKS - WIDTH), BF16)], axis=1)
     points = jnp.concatenate([points[:, CHUNK * k : CHUNK * (k + 1)] for k in range(CHUNKS)], axis=0)
-    points = dot(points, selection()).astype(BF16)
-    phases = jnp.concatenate(
-        [
-            jnp.concatenate([points[16 * k : 16 * (k + 1), 128 * b : 128 * (b + 1)] for k in range(CHUNKS)], axis=1)
-            for b in range(4)
-        ],
-        axis=0,
-    )[:, :ACROSS]
-
-    acc_c[...] = dot(phases, cos_tab[...])
-    acc_s[...] = dot(phases, sin_tab[...])
+
+    def by_phase(values, order):
+        return jnp.concatenate(
+            [
+                jnp.concatenate([values[16 * k : 16 * (k + 1), 128 * b : 128 * (b + 1)] for k in order], axis=1)
+                for b in range(4)
+            ],
+            axis=0,
+        )
+
+    ahead = by_phase(dot(points, sel_ref[...]), range(6))[:, :HALF]
+    behind = by_phase(dot(points, rev_ref[...]), range(CHUNKS - 1, -1, -1))
+    behind = pltpu.roll(behind, length // 4 + 1, 1)[:, :HALF]
+    twice = (iota((64, HALF), 1) * 8).astype(F32)
+    whole = full[:, :HALF]
+    share = jnp.where(twice < whole, 1.0, jnp.where(twice == whole, 0.5, 0.0))
+
+    acc_c[...] = dot(((ahead + behind) * share).astype(BF16), cos_tab[...])
+    acc_s[...] = dot(((ahead - behind) * share).astype(BF16), sin_tab[...])
     re, im = acc_c[48:64, :], -acc_s[48:64, :]
     for b in (2, 1, 0):
         re, im = (
@@ -173,6 +190,27 @@
             [part[0:10, 128 * s : 128 * (s + 1)] for s in range(SLOTS)] + [jnp.zeros((28, 128), F32)], axis=0
         )
         send1[:, c, :] = packed.T
+
+    def exchange(source, dest, sem, row, row_at):
+        for o_lat, o_fld in peers:
+            pltpu.make_async_remote_copy(
+                src_ref=source.at[row_at(o_lat, o_fld)],
+                dst_ref=dest.at[row],
+                send_sem=sems.at[sem],
+                recv_sem=sems.at[sem + 1],
+                device_id={"lat": o_lat, "fld": o_fld},
+                device_id_type=MESH,
+            ).start()
+        dest[row] = source[row_at(lat, fld)]
+
+    def finish(buffer, sem):
+        some = buffer.at[pl.ds(0, DEVS - 1)]
+        pltpu.make_async_copy(some, some, sems.at[sem]).wait()
+
+    by_owner = lambda a, b: a * FLD + b
+    by_group = lambda a, b: b * LAT + a
+    pl.semaphore_wait(barrier, DEVS - 1)
+    exchange(send1, recv1, 0, by_group(lat, fld), by_owner)
 
     for move in moves[4:]:
         move.wait()
@@ -223,26 +261,6 @@
     back_all = dot(spread_t, half, HIGH)
     back_all = jnp.where(((iota((64, 40), 0) >> 3) & 1) == (iota((64, 40), 1) & 1), back_all, 0.0)
 
-    def exchange(source, dest, sem, row, row_at):
-        for o_lat, o_fld in peers:
-            pltpu.make_async_remote_copy(
-                src_ref=source.at[row_at(o_lat, o_fld)],
-                dst_ref=dest.at[row],
-                send_sem=sems.at[sem],
-                recv_sem=sems.at[sem + 1],
-                device_id={"lat": o_lat, "fld": o_fld},
-                device_id_type=MESH,
-            ).start()
-        dest[row] = source[row_at(lat, fld)]
-
-    def finish(buffer, sem):
-        some = buffer.at[pl.ds(0, DEVS - 1)]
-        pltpu.make_async_copy(some, some, sems.at[sem]).wait()
-
-    by_owner = lambda a, b: a * FLD + b
-    by_group = lambda a, b: b * LAT + a
-    pl.semaphore_wait(barrier, DEVS - 1)
-    exchange(send1, recv1, 0, by_group(lat, fld), by_owner)
     finish(recv1, 1)
 
     for c in range(2):
@@ -262,7 +280,7 @@
                 total = jnp.where(block == j, rolled[j][(j - g) % 4], total)
             parts.append(total)
         gathered.append(jnp.concatenate(parts, axis=0))
-    modes_at = dot(to_all, jnp.concatenate(gathered, axis=1), HIGH).astype(BF16)
+    modes_at = dot_split(to_all, jnp.concatenate(gathered, axis=1)).astype(BF16)
 
     sums = []
     for p in range(PAIRS):
@@ -271,7 +289,7 @@
         damp_ref[p, 0:40, :] = damped
         sums.append(dot_nt(damped, leg4_ref[p]))
 
-    returned = dot(back_all, jnp.concatenate(sums, axis=1), HIGH)
+    returned = dot_split(back_all, jnp.concatenate(sums, axis=1))
     turned[...] = jnp.zeros_like(turned)
     for p in range(PAIRS):
         rolled = []
@@ -312,15 +330,30 @@
     finish(send2, 2)
 
 
-def points_kernel(spec_in, cos_tab, sin_tab, tre_ref, tim_ref, size_ref, spec_out, out_ref, sem):
-    move = pltpu.make_async_copy(spec_in, spec_out, sem)
+def points_kernel(
+    spec_in, cos_tab, sin_tab, tre_ref, tim_ref, size_ref, sel_ref, spec_out, out_ref, size_smem, sems
+):
+    move = pltpu.make_async_copy(spec_in, spec_out, sems.at[0])
     move.start()
-    length = size_ref[0:1, 0:1]
-    scale = 1.0 / jnp.sqrt(length)
-    total = dot_nt(tre_ref[...], cos_tab[...]) - dot_nt(tim_ref[...], sin_tab[...])
-    total = total * scale
-    total = jnp.where((iota((64, ACROSS), 1) * 4).astype(F32) < length, total, 0.0)
-    total = jnp.concatenate([total, jnp.zeros((64, LANES - ACROSS), F32)], axis=1).astype(BF16)
+    size = pltpu.make_async_copy(size_ref, size_smem, sems.at[1])
+    size.start()
+    flip = jnp.where(iota((128, 128), 0) + iota((128, 128), 1) == 127, 1.0, 0.0).astype(BF16)
+    even = dot_nt(tre_ref[...], cos_tab[...])
+    odd = dot_nt(tim_ref[...], sin_tab[...])
+    size.wait()
+    length = size_smem[0, 0]
+    scale = 1.0 / jnp.sqrt(jnp.full((1, HALF), length.astype(F32), F32))
+    ahead = (even - odd) * scale
+    behind = ((even + odd) * scale).astype(BF16)
+    behind = jnp.concatenate([behind, jnp.zeros((64, 768 - HALF), BF16)], axis=1)
+    behind = dot(jnp.concatenate([behind[:, 128 * k : 128 * (k + 1)] for k in range(6)], axis=0), flip)
+    behind = jnp.concatenate(
+        [jnp.zeros((64, LANES - 768), F32)] + [behind[64 * k : 64 * (k + 1)] for k in range(5, -1, -1)], axis=1
+    )
+    behind = pltpu.roll(behind, length // 4 + 1, 1)
+    ahead = jnp.concatenate([ahead, jnp.zeros((64, LANES - HALF), F32)], axis=1)
+    across = iota((64, LANES), 1)
+    total = jnp.where(across * 8 <= length, ahead, jnp.where(across * 4 < length, behind, 0.0)).astype(BF16)
     total = jnp.concatenate(
         [
             jnp.concatenate([total[16 * b : 16 * (b + 1), 128 * k : 128 * (k + 1)] for b in range(4)], axis=1)
@@ -328,16 +361,17 @@
         ],
         axis=0,
     )
-    total = dot_nt(total, selection())
+    total = dot_nt(total, sel_ref[...])
     total = jnp.concatenate([total[16 * k : 16 * (k + 1)] for k in range(CHUNKS)], axis=1)[:, :WIDTH]
     for f in range(FIELDS):
         out_ref[f, :, :] = total[2 * f : 2 * f + 2].astype(BF16)
     move.wait()
 
 
-def selection():
+def selection(flipped):
     column = iota((1, CHUNK), 1)
-    target = (column & 127) * 4 + (column >> 7)
+    across = column & 127
+    target = (127 - across if flipped else across) * 4 + (column >> 7)
     return jnp.where(iota((CHUNK, CHUNK), 0) == target, 1.0, 0.0).astype(BF16)
 
 
@@ -349,14 +383,15 @@
         send_kernel,
         out_shape=(
             pltpu.VMEM(spec_shape, F32),
-            pltpu.VMEM((ACROSS, WAVES), BF16),
-            pltpu.VMEM((ACROSS, WAVES), BF16),
+            pltpu.VMEM((HALF, WAVES), BF16),
+            pltpu.VMEM((HALF, WAVES), BF16),
             pltpu.VMEM((64, WAVES), BF16),
             pltpu.VMEM((64, WAVES), BF16),
-            pltpu.VMEM((8, 128), F32),
+            pltpu.VMEM((8, 128), I32),
+            pltpu.VMEM((CHUNK, CHUNK), BF16),
         ),
         in_specs=[pl.BlockSpec(memory_space=pltpu.HBM)] * 9,
-        out_specs=(vmem,) * 6,
+        out_specs=(vmem,) * 7,
         scratch_shapes=[
             pltpu.SMEM((LAT,), I32),
             pltpu.SMEM((LAT,), I32),
@@ -368,8 +403,9 @@
             pltpu.VMEM((ALL_FIELDS, ALL_FIELDS), F32),
             pltpu.VMEM((ALL_FIELDS, ALL_FIELDS), F32),
             pltpu.VMEM((1, ALL_FIELDS), F32),
-            pltpu.VMEM((88, WAVES), F32),
-            pltpu.VMEM((88, WAVES), F32),
+            pltpu.VMEM((48, WAVES), F32),
+            pltpu.VMEM((48, WAVES), F32),
+            pltpu.VMEM((CHUNK, CHUNK), BF16),
             pltpu.VMEM((PAIRS, 128, LANES), BF16),
             pltpu.VMEM((PAIRS, 40, LANES), F32),
             pltpu.VMEM((PAIRS, 48, LANES), BF16),
@@ -410,9 +446,9 @@
             jax.ShapeDtypeStruct(spec_shape, F32),
             jax.ShapeDtypeStruct((FIELDS, 2, WIDTH), BF16),
         ),
-        in_specs=[vmem] * 6,
+        in_specs=[vmem] * 7,
         out_specs=(anywhere, vmem),
-        scratch_shapes=[pltpu.SemaphoreType.DMA],
+        scratch_shapes=[pltpu.SMEM((8, 128), I32), pltpu.SemaphoreType.DMA((2,))],
         compiler_params=pltpu.CompilerParams(vmem_limit_bytes=24 * 1024 * 1024),
         name="to_points",
     )(*held)

time: 29.6 us -> 27.8 us (0.939)
  Pallas kernels: 28.8 us -> 27 us
    pallas_call x1, Pallas kernels: 25.9 us -> 24.6 us  [per_device(): pl.pallas_call(send_kernel, out_shape=(pltpu.VMEM(spec_shape, F32), pltpu...]
    pallas_call x1, Pallas kernels: 2.91 us -> 2.44 us  [per_device(): pl.pallas_call(points_kernel, out_shape=(jax.ShapeDtypeStruct(spec_shape,...]
where the time goes in v2:
time: 27.8 us; the launch traced here: 27.7 us
  Pallas kernels  27 us (97%)
  between operations  0.64 us (2%)
    pallas_call x1, Pallas kernels, per_device(): pl.pallas_call(send_kernel, out_shape=(pltpu.VMEM(spec_shape, F32), pltpu...  24.6 us
    pallas_call x1, Pallas kernels, per_device(): pl.pallas_call(points_kernel, out_shape=(jax.ShapeDtypeStruct(spec_shape,...  2.44 us

profile of v2, /device:TPU:1, one launch (start us, length us, event | category | flops | bytes accessed | tf_op | source)
XLA Modules:
  0.0 27.7 jit_solution(11476064595716561731)
XLA Ops:
  0.6 24.6 %to_spectral.1 = (f32[20,5,2,1281]{3,2,1,0:T(2,128)S(1)}, bf16[672,1280]{1,0:T(8,128)(2,1)S(1)}, bf16[672,1280]{1,0:T(8,128)(2,1)S(1)}, bf16[64,1280]{1,0:T(8,12...) custom-call(s32[32]{0:T(128)} %len_hbm.1, s32[32]{0:T(128)} %band_s_hbm.1, ...), custom_call_target="tpu_custom_call" | custom-call | tf_op jit(solution)/shard_map/to_spectral/pallas_call | solution.py:382
  25.2 2.4 %to_points.1 = (f32[20,5,2,1281]{3,2,1,0:T(2,128)}, bf16[5,2,5248]{2,1,0:T(2,128)(2,1)}) custom-call(f32[20,5,2,1281]{3,2,1,0:T(2,128)S(1)} %get-tuple-element.11.spec_in, bf16[672,1280]{1,0:T(8,128)(2,1)S(1)} %get-tuple-element.12.cos_tab, bf16[672,1280]{1,0:T(8,128)(2,1)S(1)} %get-tuple-element.13.sin_tab, bf16[64,1280]{1,0:T(8,128)(2,1)S(1)} %get-tuple-element.14.tre_ref, ...), custom_call_target="tpu_custom_call" | custom-call | tf_op jit(solution)/shard_map/to_points/pallas_call | solution.py:443

commit v3 on v2

--- a/solution.py
+++ b/solution.py
@@ -1,4 +1,3 @@
-import functools
 import math
 
 import jax
@@ -12,6 +11,7 @@
 MESH = pl.DeviceIdType.MESH
 F32, BF16, I32 = jnp.float32, jnp.bfloat16, jnp.int32
 NT = (((1,), (1,)), ((), ()))
+TN = (((0,), (0,)), ((), ()))
 
 LAT, FLD = 32, 4
 DEVS = LAT * FLD
@@ -25,7 +25,9 @@
 WAVES = DEVS * SLOTS
 HALF = 672
 GROUP = 256
-UNROLL = 2
+ROWS = 40
+MAIN = PLACES - 1
+UNROLL = 42
 STEP = 16
 BLOCKS = HALF // STEP
 LANES = 1408
@@ -39,6 +41,10 @@
 
 def dot(a, b, precision=None):
     return jnp.dot(a, b, precision=precision, preferred_element_type=F32)
+
+
+def dot_tn(a, b):
+    return lax.dot_general(a, b, TN, preferred_element_type=F32)
 
 
 def dot_nt(a, b):
@@ -74,10 +80,14 @@
     return upper, (value - upper.astype(F32)).astype(BF16)
 
 
-def dot_split(left, right):
-    left_upper, left_lower = split(left)
-    right_upper, right_lower = split(right)
-    return dot(left_upper, right_upper) + (dot(left_upper, right_lower) + dot(left_lower, right_upper))
+def triple(left):
+    upper, lower = split(left)
+    return jnp.concatenate([upper, upper, lower], axis=1)
+
+
+def dot_triple(left, right):
+    upper, lower = split(right)
+    return dot(left, jnp.concatenate([upper, lower, upper], axis=0))
 
 
 def offsets():
@@ -141,19 +151,6 @@
         c, s = turn((iota((8, WAVES), 0) + start).astype(F32) * (waves * float(STEP)), quarter, inv_quarter)
         wc_ref[start : start + 8, :] = c
         ws_ref[start : start + 8, :] = s
-    for start in range(0, WAVES, GROUP):
-        lanes = slice(start, start + GROUP)
-        bc, bs = base_c[:, lanes], base_s[:, lanes]
-
-        def fill(j, carry):
-            c, s = wc_ref[pl.ds(j, 1), lanes], ws_ref[pl.ds(j, 1), lanes]
-            rows = pl.ds(pl.multiple_of(j * STEP, STEP), STEP)
-            cos_tab[rows, lanes] = (bc * c - bs * s).astype(BF16)
-            sin_tab[rows, lanes] = (bs * c + bc * s).astype(BF16)
-            return carry
-
-        lax.fori_loop(0, BLOCKS, fill, 0, unroll=UNROLL)
-
     points = jnp.concatenate([grid_ref[f].astype(F32) for f in range(FIELDS)], axis=0)
     points = jnp.where(iota((2 * FIELDS, WIDTH), 1) < length, points, 0.0)
     points = jnp.concatenate([points, jnp.zeros((16 - 2 * FIELDS, WIDTH), F32)], axis=0).astype(BF16)
@@ -176,8 +173,22 @@
     whole = full[:, :HALF]
     share = jnp.where(twice < whole, 1.0, jnp.where(twice == whole, 0.5, 0.0))
 
-    acc_c[...] = dot(((ahead + behind) * share).astype(BF16), cos_tab[...])
-    acc_s[...] = dot(((ahead - behind) * share).astype(BF16), sin_tab[...])
+    plus = ((ahead + behind) * share).astype(BF16)
+    minus = ((ahead - behind) * share).astype(BF16)
+    for start in range(0, WAVES, GROUP):
+        lanes = slice(start, start + GROUP)
+        bc, bs = base_c[:, lanes], base_s[:, lanes]
+
+        def fill(j, carry):
+            c, s = wc_ref[pl.ds(j, 1), lanes], ws_ref[pl.ds(j, 1), lanes]
+            rows = pl.ds(pl.multiple_of(j * STEP, STEP), STEP)
+            cos_tab[rows, lanes] = (bc * c - bs * s).astype(BF16)
+            sin_tab[rows, lanes] = (bs * c + bc * s).astype(BF16)
+            return carry
+
+        lax.fori_loop(0, BLOCKS, fill, 0, unroll=UNROLL)
+        acc_c[:, lanes] = dot(plus, cos_tab[:, lanes])
+        acc_s[:, lanes] = dot(minus, sin_tab[:, lanes])
     re, im = acc_c[48:64, :], -acc_s[48:64, :]
     for b in (2, 1, 0):
         re, im = (
@@ -214,52 +225,59 @@
 
     for move in moves[4:]:
         move.wait()
-    perm = jnp.where(iota((LAT, LAT), 0) == band_ref[...], 1.0, 0.0).astype(BF16)
+    perm = jnp.where(iota((LAT, LAT), 0) == band_ref[...], 1.0, 0.0)
     rates = jnp.sum(
-        jnp.where((iota((40, ALL_FIELDS), 0) >> 1) == iota((40, ALL_FIELDS), 1), rate_ref[...], 0.0),
+        jnp.where((iota((ROWS, ALL_FIELDS), 0) >> 1) == iota((ROWS, ALL_FIELDS), 1), rate_ref[...], 0.0),
         axis=1, keepdims=True,
     )
-    place = iota((1, LANES), 1)
+    place = iota((1, MAIN), 1)
+    quad = iota((1, 128), 1) >> 5
+    wide_perm = jnp.concatenate([perm] * 4, axis=1).astype(BF16)
+    final = 1.0 / (1.0 + rates)
+    edges = []
+    inv_ref[ROWS * PAIRS :, :] = jnp.zeros((8, MAIN), F32)
     for p in range(PAIRS):
         first = fold_s_ref[2 * p, owner]
-        last = leg_ref[p, :, PLACES - 1 : PLACES]
-        value = jnp.concatenate(
-            [leg_ref[p, :, 0 : PLACES - 1], jnp.where(iota((LAT, 128), 1) == 0, last, 0.0)], axis=1
-        )
-        value = lax.dot_general(perm, value.astype(BF16), (((0,), (0,)), ((), ())), preferred_element_type=F32)
+        value = dot_tn(perm.astype(BF16), leg_ref[p, :, 0:MAIN].astype(BF16))
         partner = place > CUT - first
         one = jnp.where(partner, 0.0, value)
         two = jnp.where(partner, value, 0.0)
         sign_one = jnp.where((place & 1) == 1, -1.0, 1.0)
         sign_two = jnp.where(((place + first) & 1) == 1, -1.0, 1.0)
-        leg4_ref[p, 0:32, :] = one.astype(BF16)
-        leg4_ref[p, 32:64, :] = (one * sign_one).astype(BF16)
-        leg4_ref[p, 64:96, :] = two.astype(BF16)
-        leg4_ref[p, 96:128, :] = (two * sign_two).astype(BF16)
+        for k, masked in enumerate((one, one * sign_one, two, two * sign_two)):
+            leg4_ref[128 * p + 32 * k : 128 * p + 32 * (k + 1), :] = masked.astype(BF16)
         degree = jnp.where(partner, place - 1, first + place).astype(F32)
         tau = degree * (degree + 1.0) * (1.0 / float(CUT * (CUT + 1)))
-        inv_ref[p] = 1.0 / (1.0 + rates * tau)
-
-    rows, cols = iota((40, 64), 0), iota((40, 64), 1)
-    pick = jnp.where((iota((40, 20), 0) >> 1) == iota((40, 20), 1), 1.0, 0.0)
+        inv_ref[ROWS * p : ROWS * (p + 1), :] = 1.0 / (1.0 + rates * tau)
+        edge = dot_tn(leg_ref[p, :, MAIN:PLACES].astype(BF16), wide_perm)
+        odd = ((iota((1, 128), 1) * 0 + MAIN + first) & 1) == 1
+        edges.append(jnp.where(quad < 2, 0.0, jnp.where((quad == 3) & odd, -edge, edge)))
+
+    rows, cols = iota((ROWS, 64), 0), iota((ROWS, 64), 1)
+    pick = jnp.where((iota((ROWS, 20), 0) >> 1) == iota((ROWS, 20), 1), 1.0, 0.0)
     spread_col = iota((20, 64), 1)
     spread = jnp.where(
         ((spread_col & 7) < FIELDS) & (iota((20, 64), 0) == (spread_col >> 4) * FIELDS + (spread_col & 7)), 1.0, 0.0
     )
     to_all = dot(dot(pick, to_ref[...], HIGH), spread, HIGH)
-    to_all = jnp.where((rows & 1) == ((cols >> 3) & 1), to_all, 0.0)
-    pick_t = jnp.where(iota((20, 40), 0) == (iota((20, 40), 1) >> 1), 1.0, 0.0)
+    to_all = triple(jnp.where((rows & 1) == ((cols >> 3) & 1), to_all, 0.0))
+    pick_t = jnp.where(iota((20, ROWS), 0) == (iota((20, ROWS), 1) >> 1), 1.0, 0.0)
     half = dot(back_ref[...], pick_t, HIGH)
     back_rows = dot(pick, half, HIGH)
-    back_rows = jnp.where((iota((40, 40), 0) & 1) == (iota((40, 40), 1) & 1), back_rows, 0.0)
-    back_upper, back_lower = split(back_rows)
-    back_two = jnp.concatenate([back_upper.astype(F32), back_lower.astype(F32)], axis=0).astype(BF16)
+    back_rows = jnp.where((iota((ROWS, ROWS), 0) & 1) == (iota((ROWS, ROWS), 1) & 1), back_rows, 0.0)
+    blank = jnp.zeros((ROWS, ROWS), F32)
+    back_pair = jnp.concatenate(
+        [jnp.concatenate([back_rows, blank], axis=1), jnp.concatenate([blank, back_rows], axis=1)], axis=0
+    )
+    back_pair = jnp.concatenate(split(back_pair), axis=0)
+
     spread_row = iota((64, 20), 0)
     spread_t = jnp.where(
         ((spread_row & 7) < FIELDS) & (iota((64, 20), 1) == (spread_row >> 4) * FIELDS + (spread_row & 7)), 1.0, 0.0
     )
     back_all = dot(spread_t, half, HIGH)
-    back_all = jnp.where(((iota((64, 40), 0) >> 3) & 1) == (iota((64, 40), 1) & 1), back_all, 0.0)
+    back_all = jnp.where(((iota((64, ROWS), 0) >> 3) & 1) == (iota((64, ROWS), 1) & 1), back_all, 0.0)
+    back_all = triple(back_all)
 
     finish(recv1, 1)
 
@@ -280,16 +298,29 @@
                 total = jnp.where(block == j, rolled[j][(j - g) % 4], total)
             parts.append(total)
         gathered.append(jnp.concatenate(parts, axis=0))
-    modes_at = dot_split(to_all, jnp.concatenate(gathered, axis=1)).astype(BF16)
-
-    sums = []
-    for p in range(PAIRS):
-        modes = dot(modes_at[:, 128 * p : 128 * (p + 1)], leg4_ref[p])
-        damped = (modes * inv_ref[p]).astype(BF16)
-        damp_ref[p, 0:40, :] = damped
-        sums.append(dot_nt(damped, leg4_ref[p]))
-
-    returned = dot_split(back_all, jnp.concatenate(sums, axis=1))
+    modes_at = dot_triple(to_all, jnp.concatenate(gathered, axis=1))
+    nothing = jnp.zeros((ROWS, 128), F32)
+    sums, ends = [], []
+    for p in range(0, PAIRS, 2):
+        at = [modes_at[:, 128 * q : 128 * (q + 1)] if q < PAIRS else nothing for q in (p, p + 1)]
+        both = jnp.concatenate(
+            [jnp.concatenate([at[0], nothing], axis=1), jnp.concatenate([nothing, at[1]], axis=1)], axis=0
+        ).astype(BF16)
+        if p + 1 == PAIRS:
+            both = both[0:48, 0:128]
+        count = both.shape[0]
+        tables = slice(128 * p, 128 * p + both.shape[1])
+        places = inv_ref[ROWS * p : ROWS * p + count, :]
+        damped = (dot(both, leg4_ref[tables, :]) * places).astype(BF16)
+        damp_ref[p // 2, 0:count, :] = damped
+        total = dot_nt(damped, leg4_ref[tables, :])
+        for k in range(min(2, PAIRS - p)):
+            exact = at[k].astype(BF16).astype(F32)
+            end = jnp.sum(exact * edges[p + k], axis=1, keepdims=True) * final
+            ends.append(end)
+            sums.append(total[ROWS * k : ROWS * (k + 1), 128 * k : 128 * (k + 1)] + end * edges[p + k])
+
+    returned = dot_triple(back_all, jnp.concatenate(sums, axis=1))
     turned[...] = jnp.zeros_like(turned)
     for p in range(PAIRS):
         rolled = []
@@ -307,11 +338,22 @@
         send2[:, c, :] = turned[c].T
     exchange(send2, recv2, 2, by_owner(lat, fld), by_group)
 
+    lane = iota((ROWS, 128), 1)
+    last = jnp.zeros((ROWS, 128), F32)
     for p in range(PAIRS):
-        spec = dot(back_two, damp_ref[p, 0:40, :])
-        spec = spec[0:40] + spec[40:80]
-        for g in range(ALL_FIELDS):
-            spec_ref[g, p, :, :] = spec[2 * g : 2 * g + 2, 0:PLACES]
+        last = jnp.where(lane == p, ends[p], last)
+    last = dot(back_rows, last, HIGH)
+    for p in range(0, PAIRS, 2):
+        count = 2 if p + 1 < PAIRS else 1
+        depth = 2 * ROWS if count == 2 else 48
+        spec = dot(back_pair[:, 0:depth], damp_ref[p // 2, 0:depth, :])
+        spec = spec[0 : 2 * ROWS] + spec[2 * ROWS : 4 * ROWS]
+        for k in range(count):
+            block_rows = jnp.concatenate(
+                [spec[ROWS * k : ROWS * (k + 1)], last[:, p + k : p + k + 1]], axis=1
+            )
+            for g in range(ALL_FIELDS):
+                spec_ref[g, p + k, :, :] = block_rows[2 * g : 2 * g + 2]
 
     finish(recv2, 3)
 
@@ -406,9 +448,9 @@
             pltpu.VMEM((48, WAVES), F32),
             pltpu.VMEM((48, WAVES), F32),
             pltpu.VMEM((CHUNK, CHUNK), BF16),
-            pltpu.VMEM((PAIRS, 128, LANES), BF16),
-            pltpu.VMEM((PAIRS, 40, LANES), F32),
-            pltpu.VMEM((PAIRS, 48, LANES), BF16),
+            pltpu.VMEM((PAIRS * 128, MAIN), BF16),
+            pltpu.VMEM((PAIRS * ROWS + 8, MAIN), F32),
+            pltpu.VMEM(((PAIRS + 1) // 2, 2 * ROWS, MAIN), BF16),
             pltpu.VMEM((64, WAVES), F32),
             pltpu.VMEM((64, WAVES), F32),
             pltpu.VMEM((2, 128, 128), F32),

time: 27.8 us -> 27.4 us (0.986)
  Pallas kernels: 27 us -> 26.6 us
    pallas_call x1, Pallas kernels: 24.6 us -> 24.2 us  [per_device(): pl.pallas_call(send_kernel, out_shape=(pltpu.VMEM(spec_shape, F32), pltpu...]
where the time goes in v3:
time: 27.4 us; the launch traced here: 27.3 us
  Pallas kernels  26.6 us (97%)
  between operations  0.64 us (2%)
    pallas_call x1, Pallas kernels, per_device(): pl.pallas_call(send_kernel, out_shape=(pltpu.VMEM(spec_shape, F32), pltpu...  24.2 us
    pallas_call x1, Pallas kernels, per_device(): pl.pallas_call(points_kernel, out_shape=(jax.ShapeDtypeStruct(spec_shape,...  2.44 us

profile of v3, /device:TPU:1, one launch (start us, length us, event | category | flops | bytes accessed | tf_op | source)
XLA Modules:
  0.0 27.3 jit_solution(3470812666912568394)
XLA Ops:
  0.6 24.2 %to_spectral.1 = (f32[20,5,2,1281]{3,2,1,0:T(2,128)S(1)}, bf16[672,1280]{1,0:T(8,128)(2,1)S(1)}, bf16[672,1280]{1,0:T(8,128)(2,1)S(1)}, bf16[64,1280]{1,0:T(8,12...) custom-call(s32[32]{0:T(128)} %len_hbm.1, s32[32]{0:T(128)} %band_s_hbm.1, ...), custom_call_target="tpu_custom_call" | custom-call | tf_op jit(solution)/shard_map/to_spectral/pallas_call | solution.py:424
  24.8 2.4 %to_points.1 = (f32[20,5,2,1281]{3,2,1,0:T(2,128)}, bf16[5,2,5248]{2,1,0:T(2,128)(2,1)}) custom-call(f32[20,5,2,1281]{3,2,1,0:T(2,128)S(1)} %get-tuple-element.11.spec_in, bf16[672,1280]{1,0:T(8,128)(2,1)S(1)} %get-tuple-element.12.cos_tab, bf16[672,1280]{1,0:T(8,128)(2,1)S(1)} %get-tuple-element.13.sin_tab, bf16[64,1280]{1,0:T(8,128)(2,1)S(1)} %get-tuple-element.14.tre_ref, ...), custom_call_target="tpu_custom_call" | custom-call | tf_op jit(solution)/shard_map/to_points/pallas_call | solution.py:485

commit v4 on v3

--- a/solution.py
+++ b/solution.py
@@ -1,4 +1,5 @@
 import math
+import random
 
 import jax
 import jax.numpy as jnp
@@ -23,11 +24,11 @@
 CUT = 1279
 WIDTH = 5248
 WAVES = DEVS * SLOTS
-HALF = 672
+HALF = 656
 GROUP = 256
 ROWS = 40
 MAIN = PLACES - 1
-UNROLL = 42
+UNROLL = 41
 STEP = 16
 BLOCKS = HALF // STEP
 LANES = 1408
@@ -93,6 +94,7 @@
 def offsets():
     hops = (0, 1, 2, 1)
     steps = [(x, y, z, c) for y in range(4) for z in range(4) for c in range(2) for x in range(4)][1:]
+    random.Random(5).shuffle(steps)
     return sorted(steps, key=lambda step: -(hops[step[0]] + hops[step[1]] + hops[step[2]]))
 
 

time: 27.4 us -> 27 us (0.985)
  Pallas kernels: 26.6 us -> 26.3 us
where the time goes in v4:
time: 27 us; the launch traced here: 26.9 us
  Pallas kernels  26.3 us (97%)
  between operations  0.64 us (2%)
    pallas_call x1, Pallas kernels, per_device(): pl.pallas_call(send_kernel, out_shape=(pltpu.VMEM(spec_shape, F32), pltpu...  24 us
    pallas_call x1, Pallas kernels, per_device(): pl.pallas_call(points_kernel, out_shape=(jax.ShapeDtypeStruct(spec_shape,...  2.31 us

profile of v4, /device:TPU:1, one launch (start us, length us, event | category | flops | bytes accessed | tf_op | source)
XLA Modules:
  0.0 26.9 jit_solution(15115452045264411758)
XLA Ops:
  0.6 24.0 %to_spectral.1 = (f32[20,5,2,1281]{3,2,1,0:T(2,128)S(1)}, bf16[656,1280]{1,0:T(8,128)(2,1)S(1)}, bf16[656,1280]{1,0:T(8,128)(2,1)S(1)}, bf16[64,1280]{1,0:T(8,12...) custom-call(s32[32]{0:T(128)} %len_hbm.1, s32[32]{0:T(128)} %band_s_hbm.1, ...), custom_call_target="tpu_custom_call" | custom-call | tf_op jit(solution)/shard_map/to_spectral/pallas_call | solution.py:426
  24.6 2.3 %to_points.1 = (f32[20,5,2,1281]{3,2,1,0:T(2,128)}, bf16[5,2,5248]{2,1,0:T(2,128)(2,1)}) custom-call(f32[20,5,2,1281]{3,2,1,0:T(2,128)S(1)} %get-tuple-element.11.spec_in, bf16[656,1280]{1,0:T(8,128)(2,1)S(1)} %get-tuple-element.12.cos_tab, bf16[656,1280]{1,0:T(8,128)(2,1)S(1)} %get-tuple-element.13.sin_tab, bf16[64,1280]{1,0:T(8,128)(2,1)S(1)} %get-tuple-element.14.tre_ref, ...), custom_call_target="tpu_custom_call" | custom-call | tf_op jit(solution)/shard_map/to_points/pallas_call | solution.py:487

commit v5 on v4

--- a/solution.py
+++ b/solution.py
@@ -119,8 +119,6 @@
             )
         )
     ]
-    for move in moves:
-        move.start()
 
     high, middle, core = lat // 8, lax.rem(lat // 2, 4), lax.rem(lat, 2)
     xs, ys, zs_, cs = (
@@ -133,6 +131,8 @@
     for o_lat, o_fld in peers:
         pl.semaphore_signal(barrier, inc=1, device_id={"lat": o_lat, "fld": o_fld}, device_id_type=MESH)
 
+    for move in moves:
+        move.start()
     sel_ref[...] = selection(False)
     rev_ref[...] = selection(True)
 

time: 27 us -> 27.1 us (level)
  no operation moved by 1% of the time
where the time goes in v5:
time: 27.1 us; the launch traced here: 26.9 us
  Pallas kernels  26.3 us (97%)
  between operations  0.64 us (2%)
    pallas_call x1, Pallas kernels, per_device(): pl.pallas_call(send_kernel, out_shape=(pltpu.VMEM(spec_shape, F32), pltpu...  24 us
    pallas_call x1, Pallas kernels, per_device(): pl.pallas_call(points_kernel, out_shape=(jax.ShapeDtypeStruct(spec_shape,...  2.31 us

profile of v5, /device:TPU:1, one launch (start us, length us, event | category | flops | bytes accessed | tf_op | source)
XLA Modules:
  0.0 26.9 jit_solution(8591336587128078391)
XLA Ops:
  0.6 24.0 %to_spectral.1 = (f32[20,5,2,1281]{3,2,1,0:T(2,128)S(1)}, bf16[656,1280]{1,0:T(8,128)(2,1)S(1)}, bf16[656,1280]{1,0:T(8,128)(2,1)S(1)}, bf16[64,1280]{1,0:T(8,12...) custom-call(s32[32]{0:T(128)} %len_hbm.1, s32[32]{0:T(128)} %band_s_hbm.1, ...), custom_call_target="tpu_custom_call" | custom-call | tf_op jit(solution)/shard_map/to_spectral/pallas_call | solution.py:426
  24.6 2.3 %to_points.1 = (f32[20,5,2,1281]{3,2,1,0:T(2,128)}, bf16[5,2,5248]{2,1,0:T(2,128)(2,1)}) custom-call(f32[20,5,2,1281]{3,2,1,0:T(2,128)S(1)} %get-tuple-element.11.spec_in, bf16[656,1280]{1,0:T(8,128)(2,1)S(1)} %get-tuple-element.12.cos_tab, bf16[656,1280]{1,0:T(8,128)(2,1)S(1)} %get-tuple-element.13.sin_tab, bf16[64,1280]{1,0:T(8,128)(2,1)S(1)} %get-tuple-element.14.tre_ref, ...), custom_call_target="tpu_custom_call" | custom-call | tf_op jit(solution)/shard_map/to_points/pallas_call | solution.py:487
